TPU v7x, 32 devices: a whole 2x2x4 slice. The times are simulated.
32 devices in a mesh: grp: 2 (over x), rcv: 16 (over z, y, core).
Axes of the slice: x: 2, y: 2, z: 4, core: 2. Of those that a mesh axis runs over, the one named last changes fastest.
Arguments:
- reflection: bfloat16 [8, 2, 768, 768], P('grp', None, 'rcv'), parts along dimension 0, as said below
- direct_wave: float32 [32, 768, 256], P('grp', 'rcv'), parts along dimension 0, may hold values from -6 to 6
- mute_start_position: int32 [32, 768], P('grp', 'rcv'), parts along dimension 0, may hold values from 32 to 224
Outputs:
- downgoing: float32 [32, 768, 256], P('grp', 'rcv'), parts along dimension 0
- upgoing: float32 [32, 768, 256], P('grp', 'rcv'), parts along dimension 0
There are 2 independent parts, one for each index of `grp`. A program takes and returns all parts, laid end to end along the dimension named above; each array names one. Nothing has to cross between parts.
Inputs may be any that keep to these rules, and one draw needn't show every extreme that they name: reflection is reciprocal: reflection[j, c, x, y] == reflection[j, c, y, x] for every bin j, part c and positions x, y.
All inputs are finite; a program needn't handle non-finite values.
Results may differ from a plain program's by a relative error of at most 0.006.
Values may be sent and summed in bfloat16 or wider, within the bound.
A program may use at most 64 MiB of HBM per device.

v0:
```python
import math

import jax
import jax.numpy as jnp
from jax import lax
from jax.sharding import PartitionSpec as P

ITERS = 4


def fourier_tables(tick_total, bins_count):
    clock_moments = jnp.arange(tick_total, dtype=jnp.int32)
    temporal_pitches = (2 * jnp.arange(bins_count, dtype=jnp.int32) + 1) * (
        tick_total // (4 * bins_count)
    )
    rotation_argument = clock_moments[:, None] * temporal_pitches[None, :] % tick_total
    angle = rotation_argument.astype(jnp.float32) * (2.0 * math.pi / tick_total)
    return (jnp.cos(angle), jnp.sin(angle))


def to_spectrum(wavefield, harmonic_real_grid, sine_table):
    factor = harmonic_real_grid.shape[0] ** (-0.5)
    real_part = (
        jnp.einsum("pxt,tf->xfp", wavefield, harmonic_real_grid, precision=lax.Precision.HIGHEST)
        * factor
    )
    imag_part = (
        -jnp.einsum("pxt,tf->xfp", wavefield, sine_table, precision=lax.Precision.HIGHEST) * factor
    )
    stacked = jnp.concatenate([real_part, imag_part], 2)
    return stacked.astype(jnp.bfloat16)


def windowed(real_part, imag_part, mute_start_position, harmonic_real_grid, sine_table):
    factor = 3.0 / math.sqrt(harmonic_real_grid.shape[0])
    wavefield = jnp.einsum(
        "xfp,tf->pxt", real_part, harmonic_real_grid, precision=lax.Precision.HIGHEST
    )
    wavefield = (
        wavefield
        - jnp.einsum("xfp,tf->pxt", imag_part, sine_table, precision=lax.Precision.HIGHEST)
    ) * factor
    clock_moments = jnp.arange(harmonic_real_grid.shape[0], dtype=jnp.int32)
    mute_retained = clock_moments[None, None, :] < mute_start_position[:, :, None]
    return jnp.where(mute_retained, wavefield, jnp.zeros_like(wavefield))


def per_device(reflection, direct_wave, mute_start_position):
    foci_count = direct_wave.shape[0]
    harmonic_real_grid, sine_table = fourier_tables(direct_wave.shape[2], reflection.shape[0])
    downgoing = direct_wave
    upgoing = direct_wave
    for iteration in range(ITERS):
        spectra = to_spectrum(downgoing, harmonic_real_grid, sine_table)
        totals = jnp.einsum(
            "fcxy,yfd->fcxd",
            reflection,
            lax.all_gather(spectra, "rcv", axis=0, tiled=True),
            preferred_element_type=jnp.float32,
        )
        real_part = jnp.swapaxes(totals[:, 0, :, :foci_count] - totals[:, 1, :, foci_count:], 0, 1)
        imag_part = jnp.swapaxes(totals[:, 0, :, foci_count:] + totals[:, 1, :, :foci_count], 0, 1)
        upgoing = windowed(
            real_part, imag_part, mute_start_position, harmonic_real_grid, sine_table
        )
        back_spectra = to_spectrum(upgoing, harmonic_real_grid, sine_table)
        product = jnp.einsum(
            "fcxy,xfd->fcyd", reflection, back_spectra, preferred_element_type=jnp.float32
        )
        term_real = product[:, 0, :, :foci_count] + product[:, 1, :, foci_count:]
        term_imag = product[:, 0, :, foci_count:] - product[:, 1, :, :foci_count]
        joined = jnp.concatenate([term_real, term_imag], 2)
        summed = lax.psum_scatter(
            jnp.swapaxes(joined, 0, 1), "rcv", scatter_dimension=0, tiled=True
        )
        back_real = summed[:, :, :foci_count]
        back_imag = summed[:, :, foci_count:]
        downgoing = direct_wave + windowed(
            back_real, back_imag, mute_start_position, harmonic_real_grid, sine_table
        )
    return (downgoing, upgoing)


def solution(mesh):
    placed = (P("grp", None, "rcv", None), P("grp", "rcv", None), P("grp", "rcv"))
    return jax.shard_map(
        per_device,
        mesh=mesh,
        in_specs=placed,
        out_specs=(P("grp", "rcv", None), P("grp", "rcv", None)),
        check_vma=False,
    )
```

profile of v0, /device:TPU:0, one launch (start us, length us, event | category | flops | bytes accessed | tf_op | source)
XLA Modules:
  0.0 365.3 jit_solution(7342532106675671263)
XLA Ops:
  7.2 0.0 reduce-scatter.13.cloned.1.call-start
  7.2 2.5 fusion.149
  9.8 1.3 fusion.173
  11.1 0.1 copy.29
  11.2 25.5 %all_gather.12 = bf16[768,4,32]{2,1,0:T(4,128)(2,1)S(1)} all-gather(bf16[48,4,32]{2,1,0:T(4,128)(2,1)S(1)} %copy.29), channel_id=1, replica_groups=mesh['grp'=2,'rcv'=16] {'rcv'}, dimensions={0}, use_global_device_ids=true | all-gather | bytes 208896 | tf_op jit(solution)/shard_map/all_gather | solution.py:58
  36.7 0.4 convolution_bitcast_fusion.7
  37.2 0.9 fusion.106
  38.1 0.9 fusion.16
  39.1 1.3 fusion.146
  40.3 1.3 fusion.170
  41.7 0.2 convolution_bitcast_fusion.3
  42.0 0.9 copy.101
  43.0 0.0 reduce-scatter.15.cloned.1.call-start
  43.0 52.9 %reduce-scatter.13.cloned.1.call-done = f32[48,128]{1,0:T(8,128)} async-done(((f32[768,128]{1,0:T(8,128)}), f32[48,128]{1,0:T(8,128)}) %reduce-scatter.13.cloned.1.call-update) | async-done | bytes 24592
  96.0 0.8 copy.102
  96.8 0.9 fusion.70
  97.7 1.0 fusion.18
  98.7 1.3 fusion.143
  100.0 1.3 fusion.167
  101.4 0.1 copy.37
  101.5 21.7 %all_gather.13 = bf16[768,4,32]{2,1,0:T(4,128)(2,1)S(1)} all-gather(bf16[48,4,32]{2,1,0:T(4,128)(2,1)S(1)} %copy.37), channel_id=1, replica_groups=mesh['grp'=2,'rcv'=16] {'rcv'}, dimensions={0}, use_global_device_ids=true | all-gather | bytes 208896 | tf_op jit(solution)/shard_map/all_gather | solution.py:58
  123.2 0.4 convolution_bitcast_fusion.6
  123.7 0.9 fusion.103
  124.6 0.9 fusion.19
  125.5 1.3 fusion.140
  126.8 1.3 fusion.164
  128.2 0.2 convolution_bitcast_fusion.2
  128.5 0.9 copy.103
  129.5 0.0 reduce-scatter.17.cloned.1.call-start
  129.5 53.0 %reduce-scatter.15.cloned.1.call-done = f32[48,128]{1,0:T(8,128)} async-done(((f32[768,128]{1,0:T(8,128)}), f32[48,128]{1,0:T(8,128)}) %reduce-scatter.15.cloned.1.call-update) | async-done | bytes 24592
  182.5 0.8 copy.104
  183.3 0.9 fusion.67
  184.3 1.0 fusion.21
  185.2 1.3 fusion.137
  186.5 1.3 fusion.161
  187.9 0.1 copy.45
  188.0 21.6 %all_gather.14 = bf16[768,4,32]{2,1,0:T(4,128)(2,1)S(1)} all-gather(bf16[48,4,32]{2,1,0:T(4,128)(2,1)S(1)} %copy.45), channel_id=1, replica_groups=mesh['grp'=2,'rcv'=16] {'rcv'}, dimensions={0}, use_global_device_ids=true | all-gather | bytes 208896 | tf_op jit(solution)/shard_map/all_gather | solution.py:58
  209.6 0.4 convolution_bitcast_fusion.5
  210.0 0.9 fusion.100
  210.9 0.9 fusion.22
  211.9 1.3 fusion.134
  213.2 1.3 fusion.158
  214.5 0.2 convolution_bitcast_fusion.1
  214.9 0.9 copy.105
  215.8 0.3 reduce-scatter.19.cloned.1.call-start
  216.1 52.8 %reduce-scatter.17.cloned.1.call-done = f32[48,128]{1,0:T(8,128)} async-done(((f32[768,128]{1,0:T(8,128)}), f32[48,128]{1,0:T(8,128)}) %reduce-scatter.17.cloned.1.call-update) | async-done | bytes 24592
  268.9 0.8 copy.106
  269.7 0.9 fusion.64
  270.6 1.0 fusion.24
  271.6 1.3 fusion.131
  272.9 1.3 fusion.155
  274.2 0.1 copy.53
  274.3 21.6 %all_gather.15 = bf16[768,4,32]{2,1,0:T(4,128)(2,1)S(1)} all-gather(bf16[48,4,32]{2,1,0:T(4,128)(2,1)S(1)} %copy.53), channel_id=1, replica_groups=mesh['grp'=2,'rcv'=16] {'rcv'}, dimensions={0}, use_global_device_ids=true | all-gather | bytes 208896 | tf_op jit(solution)/shard_map/all_gather | solution.py:58
  295.9 0.4 convolution_bitcast_fusion.4
  296.4 0.9 fusion.97
  297.3 0.9 fusion.25
  298.2 1.3 fusion.128
  299.5 1.3 fusion.152
  300.9 0.2 convolution_bitcast_fusion
  301.2 0.9 copy.107
  302.2 53.0 %reduce-scatter.19.cloned.1.call-done = f32[48,128]{1,0:T(8,128)} async-done(((f32[768,128]{1,0:T(8,128)}), f32[48,128]{1,0:T(8,128)}) %reduce-scatter.19.cloned.1.call-update) | async-done | bytes 24592
  355.2 0.8 copy.108
  356.0 0.9 fusion.61
  356.9 1.8 fusion.27
  (52 shorter events, 0.8 us)
Async XLA Ops:
  7.2 29.6 %copy-start = (bf16[4,2,48,768]{3,2,1,0:T(8,128)(2,1)S(1)}, bf16[4,2,48,768]{3,2,1,0:T(8,128)(2,1)}, u32[]{:S(2)}) copy-start(bf16[4,2,48,768]{3,2,1,0:T(8,128)(2,1)} %param.3) | copy-start | bytes 1769476
  7.2 2.6 copy-start.1
  7.2 88.8 %reduce-scatter.13.cloned.1.call-start = ((), (), s32[]{:S(2)}) async-start(), calls=%async_computation.4 | async-start | bytes 417792
  37.2 0.9 copy-start.3
  43.0 139.5 %reduce-scatter.15.cloned.1.call-start = ((), (), s32[]{:S(2)}) async-start(), calls=%async_computation.5 | async-start | bytes 417792
  129.5 139.4 %reduce-scatter.17.cloned.1.call-start = ((), (), s32[]{:S(2)}) async-start(), calls=%async_computation.6 | async-start | bytes 417792
  215.8 139.4 %reduce-scatter.19.cloned.1.call-start = ((), (), s32[]{:S(2)}) async-start(), calls=%async_computation.7 | async-start | bytes 417792
  298.2 2.6 copy-start.2
Sparse Core Ops, SparseCore 0:
  43.1 52.8 reduce-scatter.12
  129.6 52.8 reduce-scatter.14
  215.9 52.8 reduce-scatter.16
  302.3 52.8 reduce-scatter.18
where the time goes:
time: 366 us; the launch traced here: 365 us
  waiting for transfers between devices  212 us (58%)
  blocking collectives  90.4 us (25%)
  matrix products  40.4 us (11%)
  between operations  14.2 us (4%)
  local copies, waits for them, and re-layouts  7.46 us (2%)
    unnamed x8, waiting for transfers between devices  212 us
    all_gather x4, blocking collectives, per_device(): lax.all_gather(spectra, 'rcv', axis=0, tiled=True)  90.4 us
    dot_general x8, matrix products, to_spectrum(): jnp.einsum('pxt,tf->xfp', wavefield, sine_table, precision=lax.Precision....  11.6 us
    dot_general x8, matrix products, to_spectrum(): jnp.einsum('pxt,tf->xfp', wavefield, harmonic_real_grid, precision=lax.Pr...  10.5 us
    dot_general x8, matrix products, windowed(): jnp.einsum('xfp,tf->pxt', imag_part, sine_table, precision=lax.Precision....  8.4 us
  transfers between devices with their start and end apart: 4, of which 4 were waited for; matrix products, arithmetic and copies ran while one was open for 0% of the time, Pallas kernels for 0%

commit v1 on v0

v1 whole, which is shorter than its diff:
```python
import functools
import math

import jax
import jax.numpy as jnp
from jax import lax
from jax.experimental import pallas as pl
from jax.experimental.pallas import tpu as pltpu
from jax.sharding import PartitionSpec as P

ITERS = 4
LANES = 128
NT = (((1,), (1,)), ((), ()))
TN = (((0,), (0,)), ((), ()))
MESH = pl.DeviceIdType.MESH


def tables(freqs):
    phases = 2 * freqs
    period = 2 * phases
    angle = [
        [2.0 * math.pi * ((r * (2 * j + 1)) % period) / period for j in range(freqs)]
        for r in range(phases)
    ]
    cosine = [[math.cos(a) for a in row] for row in angle]
    sine = [[math.sin(a) for a in row] for row in angle]
    return cosine, sine


def combs(rows, phases, ticks):
    row = lax.broadcasted_iota(jnp.int32, (rows, ticks), 0) % phases
    tick = lax.broadcasted_iota(jnp.int32, (rows, ticks), 1)
    sign = (1 - 2 * ((tick // phases) % 2)).astype(jnp.float32)
    return jnp.where(tick % phases == row, sign, 0.0).astype(jnp.bfloat16)


def add_up(terms):
    terms = list(terms)
    while len(terms) > 1:
        pairs = [a + b for a, b in zip(terms[::2], terms[1::2])]
        terms = pairs + ([terms[-1]] if len(terms) % 2 else [])
    return terms[0]


def iterate(
    devices, freqs, foci, rows, ticks,
    refl_ref, direct_ref, mute_ref, out_ref,
    matrix, spectra, own, other, kept, leave, arrive,
    matrix_send, matrix_recv, own_send, own_recv,
    block_send, block_recv, last_send, last_recv,
):
    chips = devices // 2
    pairs = chips // 2
    phases = 2 * freqs
    half = foci // 2
    width = 2 * rows
    deep = 2 * half
    me = lax.axis_index("rcv")
    core = me % 2
    chip = me // 2
    twin = chip * 2 + (1 - core)
    cosine, sine = tables(freqs)

    barrier = pltpu.get_barrier_semaphore()
    pl.semaphore_signal(barrier, inc=1, device_id={"rcv": twin}, device_id_type=MESH)

    def greet(d, carry):
        there = ((chip + d) % chips) * 2 + core
        pl.semaphore_signal(barrier, inc=1, device_id={"rcv": there}, device_id_type=MESH)
        return carry

    lax.fori_loop(1, chips, greet, 0)

    own[...] = jnp.zeros_like(own)
    comb = combs(2 * phases, phases, ticks)
    for p in range(foci):
        wave = direct_ref[p]
        high = wave.astype(jnp.bfloat16)
        low = (wave - high.astype(jnp.float32)).astype(jnp.bfloat16)
        sums = lax.dot_general(comb, high, NT, preferred_element_type=jnp.float32)
        sums += lax.dot_general(comb, low, NT, preferred_element_type=jnp.float32)
        own[0:phases, p, 0:rows] = sums[0:phases]
    own[phases, :, 0:rows] = mute_ref[...].astype(jnp.float32)

    pl.semaphore_wait(barrier, chips)

    own_copy = pltpu.make_async_remote_copy(
        src_ref=own.at[:, pl.ds(pl.multiple_of((1 - core) * half, 8), half), :],
        dst_ref=other,
        send_sem=own_send,
        recv_sem=own_recv,
        device_id={"rcv": twin},
        device_id_type=MESH,
    )
    own_copy.start()

    place = pl.ds(pl.multiple_of(core * rows, 16), rows)
    rest = LANES - width
    for j in range(freqs):
        for c in range(2):
            if rest:
                matrix[:, j, c, width:LANES, :] = jnp.zeros((pairs, rest, 2 * LANES), jnp.bfloat16)
            for k in range(chips):
                part = refl_ref[j, c, :, k * width : (k + 1) * width]
                if rest:
                    part = jnp.concatenate([part, jnp.zeros((rows, rest), jnp.bfloat16)], 1)
                matrix[k // 2, j, c, place, (k % 2) * LANES : (k % 2 + 1) * LANES] = part
    matrix_copy = pltpu.make_async_remote_copy(
        src_ref=matrix.at[:, :, :, place, :],
        dst_ref=matrix.at[:, :, :, place, :],
        send_sem=matrix_send,
        recv_sem=matrix_recv,
        device_id={"rcv": twin},
        device_id_type=MESH,
    )
    matrix_copy.start()

    own_copy.wait()

    def whole(a, b):
        left = jnp.where(core == 0, a, b)
        right = jnp.where(core == 0, b, a)
        return left + pltpu.roll(right, rows, 1)

    mine = pl.ds(pl.multiple_of(core * half, 8), half)
    sums = [whole(own[r, mine, :], other[r]) for r in range(phases + 1)]
    ends = sums.pop()
    counts = [jnp.floor((ends + (phases - 1 - r)) * (1.0 / phases)) for r in range(phases)]

    def to_spectrum(values, scale):
        lines = []
        for j in range(freqs):
            lines.append(add_up(values[r] * (scale * cosine[r][j]) for r in range(phases)))
            lines.append(add_up(values[r] * (-scale * sine[r][j]) for r in range(phases)))
        return lines

    def to_phases(lines, scale):
        return [
            add_up(
                lines[2 * j + c] * (scale * (cosine[r][j], -sine[r][j])[c])
                for j in range(freqs)
                for c in range(2)
            )
            for r in range(phases)
        ]

    first = to_spectrum(sums, ticks**-0.5)

    def block_copy(slot, d):
        there = ((chip + d) % chips) * 2 + core
        ours = spectra.at[slot, chip]
        return pltpu.make_async_remote_copy(
            src_ref=ours,
            dst_ref=ours,
            send_sem=block_send.at[slot, d],
            recv_sem=block_recv.at[slot, chip],
            device_id={"rcv": there},
            device_id_type=MESH,
        )

    def arrival(slot, source):
        theirs = spectra.at[slot, source]
        return pltpu.make_async_remote_copy(
            src_ref=theirs,
            dst_ref=theirs,
            send_sem=block_send.at[slot, 0],
            recv_sem=block_recv.at[slot, source],
            device_id={"rcv": me},
            device_id_type=MESH,
        )

    pair = chip // 2

    def convolve(slot, lines, sign):
        block = jnp.concatenate(lines, 0).astype(jnp.bfloat16)
        spectra[slot, chip] = block

        def send(d, carry):
            block_copy(slot, d).start()
            return carry

        lax.fori_loop(1, chips, send, 0, unroll=chips <= 8)
        arrival(slot, chip + 1 - 2 * (chip % 2)).wait_recv()

        def multiply(at, totals):
            out = []
            for j in range(freqs):
                left = jnp.concatenate(
                    [spectra[slot, 2 * at + h, deep * j : deep * (j + 1), :] for h in range(2)], 1
                )
                right = matrix[at, j].reshape(2 * LANES, 2 * LANES)
                out.append(
                    totals[j]
                    + lax.dot_general(left, right, NT, preferred_element_type=jnp.float32)
                )
            return tuple(out)

        totals = tuple(jnp.zeros((deep, 2 * LANES), jnp.float32) for _ in range(freqs))
        totals = multiply(pair, totals)

        def step(d, totals):
            at = (pair + d) % pairs
            arrival(slot, 2 * at).wait_recv()
            arrival(slot, 2 * at + 1).wait_recv()
            return multiply(at, totals)

        totals = lax.fori_loop(1, pairs, step, totals, unroll=chips <= 8)

        def sent(d, carry):
            block_copy(slot, d).wait_send()
            return carry

        lax.fori_loop(1, chips, sent, 0, unroll=chips <= 8)
        result = []
        for t in totals:
            result.append(t[0:half, 0:LANES] - sign * t[half:deep, LANES:])
            result.append(t[half:deep, 0:LANES] + sign * t[0:half, LANES:])
        return result

    matrix_copy.wait()

    def iteration(_, lines):
        up = to_phases(convolve(0, lines, 1.0), 3.0 * ticks**-0.5)
        for r in range(phases):
            kept[0, r] = up[r]
        back = to_spectrum([u * n for u, n in zip(up, counts)], ticks**-0.5)
        down = to_phases(convolve(1, back, -1.0), 3.0 * ticks**-0.5)
        for r in range(phases):
            kept[1, r] = down[r]
        change = to_spectrum([u * n for u, n in zip(down, counts)], ticks**-0.5)
        return tuple(a + b for a, b in zip(first, change))

    lax.fori_loop(0, ITERS, iteration, tuple(first))

    for u in range(2):
        for r in range(phases):
            wave = kept[u, r]
            turned = pltpu.roll(wave, LANES - rows, 1)
            out_ref[pl.ds(core * half, half), u, r, :] = jnp.where(core == 0, wave, turned)
            leave[u, r] = jnp.where(core == 0, turned, wave)
    last_copy = pltpu.make_async_remote_copy(
        src_ref=leave,
        dst_ref=arrive,
        send_sem=last_send,
        recv_sem=last_recv,
        device_id={"rcv": twin},
        device_id_type=MESH,
    )
    last_copy.start()
    last_copy.wait()
    for u in range(2):
        for r in range(phases):
            out_ref[pl.ds((1 - core) * half, half), u, r, :] = arrive[u, r]


def spread(phases, rows, ticks, count, waves_ref, direct_ref, mute_ref, down_ref, up_ref):
    foci = mute_ref.shape[0]
    base = pl.program_id(0) * count
    comb = combs(4 * phases, phases, ticks)
    ends = mute_ref[...].astype(jnp.float32).astype(jnp.bfloat16)
    lane = lax.broadcasted_iota(jnp.int32, (rows, ticks), 1).astype(jnp.float32)
    which = lax.broadcasted_iota(jnp.int32, (foci, ticks), 0)
    for i in range(count):
        pick = jnp.where(which == base + i, 1.0, 0.0).astype(jnp.bfloat16)
        end = lax.dot_general(ends, pick, TN, preferred_element_type=jnp.float32)
        inside = lane < end
        for u, ref in ((0, up_ref), (1, down_ref)):
            wave = waves_ref[i, u]
            high = wave.astype(jnp.bfloat16).astype(jnp.float32)
            mid = (wave - high).astype(jnp.bfloat16).astype(jnp.float32)
            low = wave - high - mid
            parts = jnp.concatenate([high, mid, low, jnp.zeros_like(low)], 0).astype(jnp.bfloat16)
            field = lax.dot_general(parts, comb, TN, preferred_element_type=jnp.float32)[0:rows]
            field = jnp.where(inside, field, 0.0)
            ref[i] = field if u == 0 else direct_ref[i] + field


def per_device(devices, reflection, direct_wave, mute_start_position):
    freqs = reflection.shape[0]
    foci, rows, ticks = direct_wave.shape
    chips = devices // 2
    phases = 2 * freqs
    half = foci // 2
    vmem = pl.BlockSpec(memory_space=pltpu.VMEM)
    dma = pltpu.SemaphoreType.DMA
    waves = pl.pallas_call(
        functools.partial(iterate, devices, freqs, foci, rows, ticks),
        out_shape=jax.ShapeDtypeStruct((foci, 2, phases, LANES), jnp.float32),
        in_specs=[vmem] * 3,
        out_specs=vmem,
        scratch_shapes=[
            pltpu.VMEM((chips // 2, freqs, 2, LANES, 2 * LANES), jnp.bfloat16),
            pltpu.VMEM((2, chips, 2 * freqs * half, LANES), jnp.bfloat16),
            pltpu.VMEM((phases + 1, foci, LANES), jnp.float32),
            pltpu.VMEM((phases + 1, half, LANES), jnp.float32),
            pltpu.VMEM((2, phases, half, LANES), jnp.float32),
            pltpu.VMEM((2, phases, half, LANES), jnp.float32),
            pltpu.VMEM((2, phases, half, LANES), jnp.float32),
            dma, dma, dma, dma,
            dma((2, chips)), dma((2, chips)),
            dma, dma,
        ],
        compiler_params=pltpu.CompilerParams(
            collective_id=0, has_side_effects=True, vmem_limit_bytes=48 * 2**20
        ),
    )(reflection, direct_wave, mute_start_position)
    count = 4
    return tuple(
        pl.pallas_call(
            functools.partial(spread, phases, rows, ticks, count),
            grid=(foci // count,),
            out_shape=[jax.ShapeDtypeStruct(direct_wave.shape, jnp.float32)] * 2,
            in_specs=[
                pl.BlockSpec((count, 2, phases, LANES), lambda i: (i, 0, 0, 0)),
                pl.BlockSpec((count, rows, ticks), lambda i: (i, 0, 0)),
                pl.BlockSpec((foci, rows), lambda i: (0, 0)),
            ],
            out_specs=[pl.BlockSpec((count, rows, ticks), lambda i: (i, 0, 0))] * 2,
            compiler_params=pltpu.CompilerParams(vmem_limit_bytes=16 * 2**20),
        )(waves, direct_wave, mute_start_position)
    )


def solution(mesh):
    placed = (P("grp", None, "rcv", None), P("grp", "rcv", None), P("grp", "rcv"))
    return jax.shard_map(
        functools.partial(per_device, mesh.shape["rcv"]),
        mesh=mesh,
        in_specs=placed,
        out_specs=(P("grp", "rcv", None), P("grp", "rcv", None)),
        check_vma=False,
    )
```

time: 366 us -> 58.5 us (0.16)
  waiting for transfers between devices: 212 us -> 0 us
  blocking collectives: 90.4 us -> 0 us
  Pallas kernels: 0 us -> 54.8 us
  matrix products: 40.4 us -> 0 us
  between operations: 14.2 us -> 0.65 us
  local copies, waits for them, and re-layouts: 7.46 us -> 2.89 us
    unnamed x8 -> x0, waiting for transfers between devices: 212 us -> none
    all_gather x4 -> x0, blocking collectives: 90.4 us -> none  [per_device(): lax.all_gather(spectra, 'rcv', axis=0, tiled=True)]
    pallas_call x0 -> x2, Pallas kernels: none -> 54.8 us  [the longest x1 52.2 us: per_device(): pl.pallas_call(functools.partial(iterate, devices, freqs, foci, rows, tic...]
    dot_general x40 -> x0, matrix products: 40.4 us -> none  [the longest x8 11.6 us: to_spectrum(): jnp.einsum('pxt,tf->xfp', wavefield, sine_table, precision=lax.Precision....]
    unnamed x16 -> x6, local copies, waits for them, and re-layouts: 7 us -> 2.89 us
  transfers between devices with their start and end apart: 4 -> 0, of which waited for: 4 -> 0; matrix products, arithmetic and copies ran while one was open for 0% -> 0% of each run, Pallas kernels for 0% -> 0%
where the time goes in v1:
time: 58.5 us; the launch traced here: 58.3 us
  Pallas kernels  54.8 us (94%)
  local copies, waits for them, and re-layouts  2.89 us (5%)
  between operations  0.65 us (1%)
    pallas_call x1, Pallas kernels, per_device(): pl.pallas_call(functools.partial(iterate, devices, freqs, foci, rows, tic...  52.2 us
    unnamed x6, local copies, waits for them, and re-layouts  2.89 us
    pallas_call x1, Pallas kernels, per_device(): pl.pallas_call(functools.partial(spread, phases, rows, ticks, count), gri...  2.55 us

profile of v1, /device:TPU:0, one launch (start us, length us, event | category | flops | bytes accessed | tf_op | source)
XLA Modules:
  0.0 58.3 jit_solution(9453825464528127855)
XLA Ops:
  0.6 0.0 copy-start
  0.6 1.1 %copy-done = f32[16,48,256]{2,1,0:T(8,128)S(1)} copy-done((f32[16,48,256]{2,1,0:T(8,128)S(1)}, f32[16,48,256]{2,1,0:T(8,128)}, u32[]{:S(2)}) %copy-start) | copy-done | bytes 786456
  1.8 0.0 copy-start.1
  1.8 1.1 %copy-done.1 = bf16[4,2,48,768]{3,2,1,0:T(8,128)(2,1)S(1)} copy-done((bf16[4,2,48,768]{3,2,1,0:T(8,128)(2,1)S(1)}, bf16[4,2,48,768]{3,2,1,0:T(8,128)(2,1)}, u32[]{:S(2)}) %copy-start.1) | copy-done | bytes 589848
  2.8 0.0 copy-start.2
  2.8 0.7 %copy-done.2 = s32[16,48]{1,0:T(8,128)S(1)} copy-done((s32[16,48]{1,0:T(8,128)S(1)}, s32[16,48]{1,0:T(8,128)}, u32[]{:S(2)}) %copy-start.2) | copy-done | bytes 3096
  3.5 52.2 %shard_map.50.waves_ref = f32[16,2,8,128]{3,2,1,0:T(8,128)S(1)} custom-call(bf16[4,2,48,768]{3,2,1,0:T(8,128)(2,1)S(1)} %copy-done.1, f32[16,48,256]{2,1,0:T(8,128)S(1)} %copy-done, s32[16,48]{1,0:T(8,128)S(1)} %copy-done.2), custom_call_target="tpu_custom_call" | custom-call | tf_op jit(solution)/shard_map/pallas_call | solution.py:286
  55.7 2.5 %shard_map.51 = (f32[16,48,256]{2,1,0:T(8,128)}, f32[16,48,256]{2,1,0:T(8,128)}) custom-call(f32[16,2,8,128]{3,2,1,0:T(8,128)S(1)} %shard_map.50.waves_ref, f32[16,48,256]{2,1,0:T(8,128)S(1)} %copy-done, s32[16,48]{1,0:T(8,128)S(1)} %copy-done.2), custom_call_target="tpu_custom_call" | custom-call | tf_op jit(solution)/shard_map/pallas_call | solution.py:309
Async XLA Ops:
  0.6 1.1 %copy-start = (f32[16,48,256]{2,1,0:T(8,128)S(1)}, f32[16,48,256]{2,1,0:T(8,128)}, u32[]{:S(2)}) copy-start(f32[16,48,256]{2,1,0:T(8,128)} %direct_ref.3) | copy-start | bytes 2359300
  1.8 1.1 %copy-start.1 = (bf16[4,2,48,768]{3,2,1,0:T(8,128)(2,1)S(1)}, bf16[4,2,48,768]{3,2,1,0:T(8,128)(2,1)}, u32[]{:S(2)}) copy-start(bf16[4,2,48,768]{3,2,1,0:T(8,128)(2,1)} %refl_ref.1) | copy-start | bytes 1769476
  2.8 0.7 %copy-start.2 = (s32[16,48]{1,0:T(8,128)S(1)}, s32[16,48]{1,0:T(8,128)}, u32[]{:S(2)}) copy-start(s32[16,48]{1,0:T(8,128)} %mute_ref.3) | copy-start | bytes 9220

commit v2 on v1

--- a/solution.py
+++ b/solution.py
@@ -44,9 +44,9 @@
 
 def iterate(
     devices, freqs, foci, rows, ticks,
-    refl_ref, direct_ref, mute_ref, out_ref,
-    matrix, spectra, own, other, kept, leave, arrive,
-    matrix_send, matrix_recv, own_send, own_recv,
+    refl_hbm, direct_hbm, mute_hbm, out_ref,
+    refl_ref, direct_ref, mute_ref, matrix, spectra, own, other, leave, arrive,
+    fetched, matrix_send, matrix_recv, own_send, own_recv,
     block_send, block_recv, last_send, last_recv,
 ):
     chips = devices // 2
@@ -61,6 +61,17 @@
     twin = chip * 2 + (1 - core)
     cosine, sine = tables(freqs)
 
+    theirs_half = pl.ds((1 - core) * half, half)
+    ours_half = pl.ds(core * half, half)
+    fetches = [
+        pltpu.make_async_copy(direct_hbm.at[theirs_half], direct_ref.at[theirs_half], fetched.at[0]),
+        pltpu.make_async_copy(mute_hbm, mute_ref, fetched.at[1]),
+        pltpu.make_async_copy(direct_hbm.at[ours_half], direct_ref.at[ours_half], fetched.at[2]),
+        pltpu.make_async_copy(refl_hbm, refl_ref, fetched.at[3]),
+    ]
+    for fetch in fetches:
+        fetch.start()
+
     barrier = pltpu.get_barrier_semaphore()
     pl.semaphore_signal(barrier, inc=1, device_id={"rcv": twin}, device_id_type=MESH)
 
@@ -73,13 +84,20 @@
 
     own[...] = jnp.zeros_like(own)
     comb = combs(2 * phases, phases, ticks)
-    for p in range(foci):
-        wave = direct_ref[p]
-        high = wave.astype(jnp.bfloat16)
-        low = (wave - high.astype(jnp.float32)).astype(jnp.bfloat16)
-        sums = lax.dot_general(comb, high, NT, preferred_element_type=jnp.float32)
-        sums += lax.dot_general(comb, low, NT, preferred_element_type=jnp.float32)
-        own[0:phases, p, 0:rows] = sums[0:phases]
+
+    def sum_phases(start):
+        for i in range(half):
+            p = start + i
+            wave = direct_ref[p]
+            high = wave.astype(jnp.bfloat16)
+            low = (wave - high.astype(jnp.float32)).astype(jnp.bfloat16)
+            sums = lax.dot_general(comb, high, NT, preferred_element_type=jnp.float32)
+            sums += lax.dot_general(comb, low, NT, preferred_element_type=jnp.float32)
+            own[0:phases, p, 0:rows] = sums[0:phases]
+
+    fetches[0].wait()
+    sum_phases((1 - core) * half)
+    fetches[1].wait()
     own[phases, :, 0:rows] = mute_ref[...].astype(jnp.float32)
 
     pl.semaphore_wait(barrier, chips)
@@ -93,6 +111,9 @@
         device_id_type=MESH,
     )
     own_copy.start()
+    fetches[2].wait()
+    sum_phases(core * half)
+    fetches[3].wait()
 
     place = pl.ds(pl.multiple_of(core * rows, 16), rows)
     rest = LANES - width
@@ -146,8 +167,26 @@
 
     first = to_spectrum(sums, ticks**-0.5)
 
+    small = chips == 8
+
+    def partner(number, d):
+        if not small:
+            return (number + d) % chips
+        flipped = 0
+        for bit in (4, 2, 1):
+            now = (number // bit) % 2
+            flipped += bit * (1 - now if d & bit else now)
+        return flipped
+
+    def each_partner(body):
+        if small:
+            for d in range(chips - 1, 0, -1):
+                body(d, 0)
+        else:
+            lax.fori_loop(1, chips, body, 0)
+
     def block_copy(slot, d):
-        there = ((chip + d) % chips) * 2 + core
+        there = partner(chip, d) * 2 + core
         ours = spectra.at[slot, chip]
         return pltpu.make_async_remote_copy(
             src_ref=ours,
@@ -171,7 +210,7 @@
 
     pair = chip // 2
 
-    def convolve(slot, lines, sign):
+    def convolve(slot, lines, sign, meanwhile=None):
         block = jnp.concatenate(lines, 0).astype(jnp.bfloat16)
         spectra[slot, chip] = block
 
@@ -179,7 +218,9 @@
             block_copy(slot, d).start()
             return carry
 
-        lax.fori_loop(1, chips, send, 0, unroll=chips <= 8)
+        each_partner(send)
+        if meanwhile is not None:
+            meanwhile()
         arrival(slot, chip + 1 - 2 * (chip % 2)).wait_recv()
 
         def multiply(at, totals):
@@ -199,58 +240,65 @@
         totals = multiply(pair, totals)
 
         def step(d, totals):
-            at = (pair + d) % pairs
+            at = partner(chip, 2 * d) // 2 if small else (pair + d) % pairs
             arrival(slot, 2 * at).wait_recv()
             arrival(slot, 2 * at + 1).wait_recv()
             return multiply(at, totals)
 
-        totals = lax.fori_loop(1, pairs, step, totals, unroll=chips <= 8)
+        if small:
+            for d in range(1, pairs):
+                totals = step(d, totals)
+        else:
+            totals = lax.fori_loop(1, pairs, step, totals)
 
         def sent(d, carry):
             block_copy(slot, d).wait_send()
             return carry
 
-        lax.fori_loop(1, chips, sent, 0, unroll=chips <= 8)
+        each_partner(sent)
         result = []
         for t in totals:
             result.append(t[0:half, 0:LANES] - sign * t[half:deep, LANES:])
             result.append(t[half:deep, 0:LANES] + sign * t[0:half, LANES:])
         return result
 
-    matrix_copy.wait()
-
-    def iteration(_, lines):
-        up = to_phases(convolve(0, lines, 1.0), 3.0 * ticks**-0.5)
+    def last_copy(u):
+        return pltpu.make_async_remote_copy(
+            src_ref=leave.at[u],
+            dst_ref=arrive.at[u],
+            send_sem=last_send.at[u],
+            recv_sem=last_recv.at[u],
+            device_id={"rcv": twin},
+            device_id_type=MESH,
+        )
+
+    def hand_over(u, waves):
+        turned = [pltpu.roll(wave, LANES - rows, 1) for wave in waves]
         for r in range(phases):
-            kept[0, r] = up[r]
+            leave[u, r] = jnp.where(core == 0, turned[r], waves[r])
+        last_copy(u).start()
+        for r in range(phases):
+            out_ref[ours_half, u, r, :] = jnp.where(core == 0, waves[r], turned[r])
+
+    def take_over(u):
+        last_copy(u).wait()
+        for r in range(phases):
+            out_ref[theirs_half, u, r, :] = arrive[u, r]
+
+    lines = first
+    for iteration in range(ITERS):
+        last = iteration == ITERS - 1
+        forward = convolve(0, lines, 1.0, None if iteration else matrix_copy.wait)
+        up = to_phases(forward, 3.0 * ticks**-0.5)
         back = to_spectrum([u * n for u, n in zip(up, counts)], ticks**-0.5)
-        down = to_phases(convolve(1, back, -1.0), 3.0 * ticks**-0.5)
-        for r in range(phases):
-            kept[1, r] = down[r]
-        change = to_spectrum([u * n for u, n in zip(down, counts)], ticks**-0.5)
-        return tuple(a + b for a, b in zip(first, change))
-
-    lax.fori_loop(0, ITERS, iteration, tuple(first))
-
-    for u in range(2):
-        for r in range(phases):
-            wave = kept[u, r]
-            turned = pltpu.roll(wave, LANES - rows, 1)
-            out_ref[pl.ds(core * half, half), u, r, :] = jnp.where(core == 0, wave, turned)
-            leave[u, r] = jnp.where(core == 0, turned, wave)
-    last_copy = pltpu.make_async_remote_copy(
-        src_ref=leave,
-        dst_ref=arrive,
-        send_sem=last_send,
-        recv_sem=last_recv,
-        device_id={"rcv": twin},
-        device_id_type=MESH,
-    )
-    last_copy.start()
-    last_copy.wait()
-    for u in range(2):
-        for r in range(phases):
-            out_ref[pl.ds((1 - core) * half, half), u, r, :] = arrive[u, r]
+        adjoint = convolve(1, back, -1.0, functools.partial(hand_over, 0, up) if last else None)
+        down = to_phases(adjoint, 3.0 * ticks**-0.5)
+        if not last:
+            change = to_spectrum([u * n for u, n in zip(down, counts)], ticks**-0.5)
+            lines = [a + b for a, b in zip(first, change)]
+    hand_over(1, down)
+    take_over(0)
+    take_over(1)
 
 
 def spread(phases, rows, ticks, count, waves_ref, direct_ref, mute_ref, down_ref, up_ref):
@@ -286,19 +334,21 @@
     waves = pl.pallas_call(
         functools.partial(iterate, devices, freqs, foci, rows, ticks),
         out_shape=jax.ShapeDtypeStruct((foci, 2, phases, LANES), jnp.float32),
-        in_specs=[vmem] * 3,
+        in_specs=[pl.BlockSpec(memory_space=pl.ANY)] * 3,
         out_specs=vmem,
         scratch_shapes=[
+            pltpu.VMEM(reflection.shape, jnp.bfloat16),
+            pltpu.VMEM(direct_wave.shape, jnp.float32),
+            pltpu.VMEM(mute_start_position.shape, jnp.int32),
             pltpu.VMEM((chips // 2, freqs, 2, LANES, 2 * LANES), jnp.bfloat16),
             pltpu.VMEM((2, chips, 2 * freqs * half, LANES), jnp.bfloat16),
             pltpu.VMEM((phases + 1, foci, LANES), jnp.float32),
             pltpu.VMEM((phases + 1, half, LANES), jnp.float32),
             pltpu.VMEM((2, phases, half, LANES), jnp.float32),
             pltpu.VMEM((2, phases, half, LANES), jnp.float32),
-            pltpu.VMEM((2, phases, half, LANES), jnp.float32),
-            dma, dma, dma, dma,
+            dma((4,)), dma, dma, dma, dma,
             dma((2, chips)), dma((2, chips)),
-            dma, dma,
+            dma((2,)), dma((2,)),
         ],
         compiler_params=pltpu.CompilerParams(
             collective_id=0, has_side_effects=True, vmem_limit_bytes=48 * 2**20

time: 58.5 us -> 56.2 us (0.961)
  Pallas kernels: 54.8 us -> 52.4 us
    pallas_call x1, Pallas kernels: 52.2 us -> 49.9 us  [per_device(): pl.pallas_call(functools.partial(iterate, devices, freqs, foci, rows, tic...]
where the time goes in v2:
time: 56.2 us; the launch traced here: 56 us
  Pallas kernels  52.4 us (93%)
  local copies, waits for them, and re-layouts  2.89 us (5%)
  between operations  0.65 us (1%)
    pallas_call x1, Pallas kernels, per_device(): pl.pallas_call(functools.partial(iterate, devices, freqs, foci, rows, tic...  49.9 us
    unnamed x6, local copies, waits for them, and re-layouts  2.89 us
    pallas_call x1, Pallas kernels, per_device(): pl.pallas_call(functools.partial(spread, phases, rows, ticks, count), gri...  2.55 us

profile of v2, /device:TPU:0, one launch (start us, length us, event | category | flops | bytes accessed | tf_op | source)
XLA Modules:
  0.0 56.0 jit_solution(4144208992435070009)
XLA Ops:
  0.6 0.0 copy-start
  0.6 1.1 %copy-done = f32[16,48,256]{2,1,0:T(8,128)S(1)} copy-done((f32[16,48,256]{2,1,0:T(8,128)S(1)}, f32[16,48,256]{2,1,0:T(8,128)}, u32[]{:S(2)}) %copy-start) | copy-done | bytes 786456
  1.8 0.0 copy-start.1
  1.8 1.1 %copy-done.1 = bf16[4,2,48,768]{3,2,1,0:T(8,128)(2,1)S(1)} copy-done((bf16[4,2,48,768]{3,2,1,0:T(8,128)(2,1)S(1)}, bf16[4,2,48,768]{3,2,1,0:T(8,128)(2,1)}, u32[]{:S(2)}) %copy-start.1) | copy-done | bytes 589848
  2.8 0.0 copy-start.2
  2.8 0.7 %copy-done.2 = s32[16,48]{1,0:T(8,128)S(1)} copy-done((s32[16,48]{1,0:T(8,128)S(1)}, s32[16,48]{1,0:T(8,128)}, u32[]{:S(2)}) %copy-start.2) | copy-done | bytes 3096
  3.5 49.9 %shard_map.50.waves_ref = f32[16,2,8,128]{3,2,1,0:T(8,128)S(1)} custom-call(bf16[4,2,48,768]{3,2,1,0:T(8,128)(2,1)S(1)} %copy-done.1, f32[16,48,256]{2,1,0:T(8,128)S(1)} %copy-done, s32[16,48]{1,0:T(8,128)S(1)} %copy-done.2), custom_call_target="tpu_custom_call" | custom-call | tf_op jit(solution)/shard_map/pallas_call | solution.py:334
  53.4 2.5 %shard_map.51 = (f32[16,48,256]{2,1,0:T(8,128)}, f32[16,48,256]{2,1,0:T(8,128)}) custom-call(f32[16,2,8,128]{3,2,1,0:T(8,128)S(1)} %shard_map.50.waves_ref, f32[16,48,256]{2,1,0:T(8,128)S(1)} %copy-done, s32[16,48]{1,0:T(8,128)S(1)} %copy-done.2), custom_call_target="tpu_custom_call" | custom-call | tf_op jit(solution)/shard_map/pallas_call | solution.py:359
Async XLA Ops:
  0.6 1.1 %copy-start = (f32[16,48,256]{2,1,0:T(8,128)S(1)}, f32[16,48,256]{2,1,0:T(8,128)}, u32[]{:S(2)}) copy-start(f32[16,48,256]{2,1,0:T(8,128)} %direct_ref.1) | copy-start | bytes 2359300
  1.8 1.1 %copy-start.1 = (bf16[4,2,48,768]{3,2,1,0:T(8,128)(2,1)S(1)}, bf16[4,2,48,768]{3,2,1,0:T(8,128)(2,1)}, u32[]{:S(2)}) copy-start(bf16[4,2,48,768]{3,2,1,0:T(8,128)(2,1)} %refl_hbm.1) | copy-start | bytes 1769476
  2.8 0.7 %copy-start.2 = (s32[16,48]{1,0:T(8,128)S(1)}, s32[16,48]{1,0:T(8,128)}, u32[]{:S(2)}) copy-start(s32[16,48]{1,0:T(8,128)} %mute_ref.1) | copy-start | bytes 9220

commit v3 on v2

--- a/solution.py
+++ b/solution.py
@@ -351,10 +351,10 @@
             dma((2,)), dma((2,)),
         ],
         compiler_params=pltpu.CompilerParams(
-            collective_id=0, has_side_effects=True, vmem_limit_bytes=48 * 2**20
+            collective_id=0, has_side_effects=True, vmem_limit_bytes=60 * 2**20
         ),
     )(reflection, direct_wave, mute_start_position)
-    count = 4
+    count = 8
     return tuple(
         pl.pallas_call(
             functools.partial(spread, phases, rows, ticks, count),

time: 56.2 us -> 53.7 us (0.956)
  local copies, waits for them, and re-layouts: 2.89 us -> 0.91 us
    unnamed x6, local copies, waits for them, and re-layouts: 2.89 us -> 0.91 us
    pallas_call x1, Pallas kernels: 2.55 us -> 1.92 us  [per_device(): pl.pallas_call(functools.partial(spread, phases, rows, ticks, count), gri...]
where the time goes in v3:
time: 53.7 us; the launch traced here: 53.6 us
  Pallas kernels  52 us (97%)
  local copies, waits for them, and re-layouts  0.91 us (2%)
  between operations  0.68 us (1%)
    pallas_call x1, Pallas kernels, per_device(): pl.pallas_call(functools.partial(iterate, devices, freqs, foci, rows, tic...  50.1 us
    pallas_call x1, Pallas kernels, per_device(): pl.pallas_call(functools.partial(spread, phases, rows, ticks, count), gri...  1.92 us

profile of v3, /device:TPU:0, one launch (start us, length us, event | category | flops | bytes accessed | tf_op | source)
XLA Modules:
  0.0 53.6 jit_solution(1041433841774519883)
XLA Ops:
  0.6 0.0 copy-start.2
  0.6 0.0 copy-start
  0.6 50.1 %shard_map.50.waves_ref = f32[16,2,8,128]{3,2,1,0:T(8,128)} custom-call(bf16[4,2,48,768]{3,2,1,0:T(8,128)(2,1)} %refl_hbm.1, f32[16,48,256]{2,1,0:T(8,128)} %direct_ref.1, s32[16,48]{1,0:T(8,128)} %mute_ref.1), custom_call_target="tpu_custom_call" | custom-call | tf_op jit(solution)/shard_map/pallas_call | solution.py:334
  50.7 0.0 copy-done.2
  50.8 0.0 copy-done
  50.8 0.0 copy-start.1
  50.8 0.9 %copy-done.1 = f32[16,2,8,128]{3,2,1,0:T(8,128)S(1)} copy-done((f32[16,2,8,128]{3,2,1,0:T(8,128)S(1)}, f32[16,2,8,128]{3,2,1,0:T(8,128)}, u32[]{:S(2)}) %copy-start.1) | copy-done | bytes 131096
  51.7 1.9 %shard_map.51 = (f32[16,48,256]{2,1,0:T(8,128)}, f32[16,48,256]{2,1,0:T(8,128)}) custom-call(f32[16,2,8,128]{3,2,1,0:T(8,128)S(1)} %copy-done.1, f32[16,48,256]{2,1,0:T(8,128)S(1)} %copy-done, s32[16,48]{1,0:T(8,128)S(1)} %copy-done.2), custom_call_target="tpu_custom_call" | custom-call | tf_op jit(solution)/shard_map/pallas_call | solution.py:359
Async XLA Ops:
  0.6 50.1 %copy-start.2 = (s32[16,48]{1,0:T(8,128)S(1)}, s32[16,48]{1,0:T(8,128)}, u32[]{:S(2)}) copy-start(s32[16,48]{1,0:T(8,128)} %mute_ref.1) | copy-start | bytes 9220
  0.6 50.1 %copy-start = (f32[16,48,256]{2,1,0:T(8,128)S(1)}, f32[16,48,256]{2,1,0:T(8,128)}, u32[]{:S(2)}) copy-start(f32[16,48,256]{2,1,0:T(8,128)} %direct_ref.1) | copy-start | bytes 2359300
  50.8 0.9 %copy-start.1 = (f32[16,2,8,128]{3,2,1,0:T(8,128)S(1)}, f32[16,2,8,128]{3,2,1,0:T(8,128)}, u32[]{:S(2)}) copy-start(f32[16,2,8,128]{3,2,1,0:T(8,128)} %shard_map.50.waves_ref) | copy-start | bytes 393220

commit v4 on v3

--- a/solution.py
+++ b/solution.py
@@ -169,14 +169,16 @@
 
     small = chips == 8
 
+    def line(d):
+        upper = (chip // 2) // 2
+        lower = (chip // 2) % 2
+        return (chip // 2, 2 * upper + 1 - lower, 2 - upper, 3 * (1 - upper))[d]
+
     def partner(number, d):
         if not small:
             return (number + d) % chips
-        flipped = 0
-        for bit in (4, 2, 1):
-            now = (number // bit) % 2
-            flipped += bit * (1 - now if d & bit else now)
-        return flipped
+        side = chip % 2
+        return 2 * line(d // 2) + (1 - side if d % 2 else side)
 
     def each_partner(body):
         if small:
@@ -209,13 +211,25 @@
         )
 
     pair = chip // 2
+    packed = spectra.shape[2] < freqs * deep
 
     def convolve(slot, lines, sign, meanwhile=None):
-        block = jnp.concatenate(lines, 0).astype(jnp.bfloat16)
-        spectra[slot, chip] = block
+        tiles = [jnp.concatenate(lines[2 * j : 2 * j + 2], 0) for j in range(freqs)]
+        if packed:
+            spare = tiles.pop()
+            lane = lax.broadcasted_iota(jnp.int32, spare.shape, 1)
+            tiles = [
+                jnp.where(lane < width, tile, pltpu.roll(spare, width - rest * i, 1))
+                for i, tile in enumerate(tiles)
+            ]
+        spectra[slot, chip] = jnp.concatenate(tiles, 0).astype(jnp.bfloat16)
 
         def send(d, carry):
             block_copy(slot, d).start()
+            return carry
+
+        def sent(d, carry):
+            block_copy(slot, d).wait_send()
             return carry
 
         each_partner(send)
@@ -223,12 +237,23 @@
             meanwhile()
         arrival(slot, chip + 1 - 2 * (chip % 2)).wait_recv()
 
+        def unpack(source):
+            held = spectra.shape[2] // deep
+            tiles = [spectra[slot, source, deep * j : deep * (j + 1), :] for j in range(held)]
+            if packed:
+                lane = lax.broadcasted_iota(jnp.int32, (deep, LANES), 1)
+                spare = None
+                for i in range(held - 1, -1, -1):
+                    piece = pltpu.roll(tiles[i].astype(jnp.float32), LANES - width + rest * i, 1)
+                    spare = piece if spare is None else jnp.where(lane < rest * (i + 1), piece, spare)
+                tiles.append(spare.astype(jnp.bfloat16))
+            return tiles
+
         def multiply(at, totals):
             out = []
+            sides = [unpack(2 * at), unpack(2 * at + 1)]
             for j in range(freqs):
-                left = jnp.concatenate(
-                    [spectra[slot, 2 * at + h, deep * j : deep * (j + 1), :] for h in range(2)], 1
-                )
+                left = jnp.concatenate([side[j] for side in sides], 1)
                 right = matrix[at, j].reshape(2 * LANES, 2 * LANES)
                 out.append(
                     totals[j]
@@ -240,22 +265,20 @@
         totals = multiply(pair, totals)
 
         def step(d, totals):
-            at = partner(chip, 2 * d) // 2 if small else (pair + d) % pairs
+            at = line(d) if small else (pair + d) % pairs
             arrival(slot, 2 * at).wait_recv()
             arrival(slot, 2 * at + 1).wait_recv()
             return multiply(at, totals)
 
         if small:
             for d in range(1, pairs):
+                if d == pairs - 1:
+                    each_partner(sent)
                 totals = step(d, totals)
         else:
             totals = lax.fori_loop(1, pairs, step, totals)
-
-        def sent(d, carry):
-            block_copy(slot, d).wait_send()
-            return carry
-
-        each_partner(sent)
+            each_partner(sent)
+
         result = []
         for t in totals:
             result.append(t[0:half, 0:LANES] - sign * t[half:deep, LANES:])
@@ -329,6 +352,8 @@
     chips = devices // 2
     phases = 2 * freqs
     half = foci // 2
+    rest = LANES - 2 * rows
+    packed = int(rest > 0 and rest * (freqs - 1) == 2 * rows)
     vmem = pl.BlockSpec(memory_space=pltpu.VMEM)
     dma = pltpu.SemaphoreType.DMA
     waves = pl.pallas_call(
@@ -341,7 +366,7 @@
             pltpu.VMEM(direct_wave.shape, jnp.float32),
             pltpu.VMEM(mute_start_position.shape, jnp.int32),
             pltpu.VMEM((chips // 2, freqs, 2, LANES, 2 * LANES), jnp.bfloat16),
-            pltpu.VMEM((2, chips, 2 * freqs * half, LANES), jnp.bfloat16),
+            pltpu.VMEM((2, chips, 2 * half * (freqs - packed), LANES), jnp.bfloat16),
             pltpu.VMEM((phases + 1, foci, LANES), jnp.float32),
             pltpu.VMEM((phases + 1, half, LANES), jnp.float32),
             pltpu.VMEM((2, phases, half, LANES), jnp.float32),

time: 53.7 us -> 49.7 us (0.926)
  Pallas kernels: 52 us -> 48 us
    pallas_call x1, Pallas kernels: 50.1 us -> 46 us  [per_device(): pl.pallas_call(functools.partial(iterate, devices, freqs, foci, rows, tic...]
where the time goes in v4:
time: 49.7 us; the launch traced here: 49.5 us
  Pallas kernels  48 us (97%)
  local copies, waits for them, and re-layouts  0.91 us (2%)
  between operations  0.68 us (1%)
    pallas_call x1, Pallas kernels, per_device(): pl.pallas_call(functools.partial(iterate, devices, freqs, foci, rows, tic...  46 us
    pallas_call x1, Pallas kernels, per_device(): pl.pallas_call(functools.partial(spread, phases, rows, ticks, count), gri...  1.92 us

profile of v4, /device:TPU:0, one launch (start us, length us, event | category | flops | bytes accessed | tf_op | source)
XLA Modules:
  0.0 49.5 jit_solution(14411503977147241194)
XLA Ops:
  0.6 0.0 copy-start.2
  0.6 0.0 copy-start
  0.6 46.0 %shard_map.50.waves_ref = f32[16,2,8,128]{3,2,1,0:T(8,128)} custom-call(bf16[4,2,48,768]{3,2,1,0:T(8,128)(2,1)} %refl_hbm.1, f32[16,48,256]{2,1,0:T(8,128)} %direct_ref.1, s32[16,48]{1,0:T(8,128)} %mute_ref.1), custom_call_target="tpu_custom_call" | custom-call | tf_op jit(solution)/shard_map/pallas_call | solution.py:359
  46.7 0.0 copy-done.2
  46.7 0.0 copy-done
  46.7 0.0 copy-start.1
  46.7 0.9 %copy-done.1 = f32[16,2,8,128]{3,2,1,0:T(8,128)S(1)} copy-done((f32[16,2,8,128]{3,2,1,0:T(8,128)S(1)}, f32[16,2,8,128]{3,2,1,0:T(8,128)}, u32[]{:S(2)}) %copy-start.1) | copy-done | bytes 131096
  47.6 1.9 %shard_map.51 = (f32[16,48,256]{2,1,0:T(8,128)}, f32[16,48,256]{2,1,0:T(8,128)}) custom-call(f32[16,2,8,128]{3,2,1,0:T(8,128)S(1)} %copy-done.1, f32[16,48,256]{2,1,0:T(8,128)S(1)} %copy-done, s32[16,48]{1,0:T(8,128)S(1)} %copy-done.2), custom_call_target="tpu_custom_call" | custom-call | tf_op jit(solution)/shard_map/pallas_call | solution.py:384
Async XLA Ops:
  0.6 46.1 %copy-start.2 = (s32[16,48]{1,0:T(8,128)S(1)}, s32[16,48]{1,0:T(8,128)}, u32[]{:S(2)}) copy-start(s32[16,48]{1,0:T(8,128)} %mute_ref.1) | copy-start | bytes 9220
  0.6 46.1 %copy-start = (f32[16,48,256]{2,1,0:T(8,128)S(1)}, f32[16,48,256]{2,1,0:T(8,128)}, u32[]{:S(2)}) copy-start(f32[16,48,256]{2,1,0:T(8,128)} %direct_ref.1) | copy-start | bytes 2359300
  46.7 0.9 %copy-start.1 = (f32[16,2,8,128]{3,2,1,0:T(8,128)S(1)}, f32[16,2,8,128]{3,2,1,0:T(8,128)}, u32[]{:S(2)}) copy-start(f32[16,2,8,128]{3,2,1,0:T(8,128)} %shard_map.50.waves_ref) | copy-start | bytes 393220

commit v5 on v4

--- a/solution.py
+++ b/solution.py
@@ -55,6 +55,7 @@
     half = foci // 2
     width = 2 * rows
     deep = 2 * half
+    rest = LANES - width
     me = lax.axis_index("rcv")
     core = me % 2
     chip = me // 2
@@ -113,28 +114,30 @@
     own_copy.start()
     fetches[2].wait()
     sum_phases(core * half)
-    fetches[3].wait()
-
-    place = pl.ds(pl.multiple_of(core * rows, 16), rows)
-    rest = LANES - width
-    for j in range(freqs):
-        for c in range(2):
-            if rest:
-                matrix[:, j, c, width:LANES, :] = jnp.zeros((pairs, rest, 2 * LANES), jnp.bfloat16)
-            for k in range(chips):
-                part = refl_ref[j, c, :, k * width : (k + 1) * width]
+
+
+    def lay_out():
+        fetches[3].wait()
+        place = pl.ds(pl.multiple_of(core * rows, 16), rows)
+        for j in range(freqs):
+            for c in range(2):
                 if rest:
-                    part = jnp.concatenate([part, jnp.zeros((rows, rest), jnp.bfloat16)], 1)
-                matrix[k // 2, j, c, place, (k % 2) * LANES : (k % 2 + 1) * LANES] = part
-    matrix_copy = pltpu.make_async_remote_copy(
-        src_ref=matrix.at[:, :, :, place, :],
-        dst_ref=matrix.at[:, :, :, place, :],
-        send_sem=matrix_send,
-        recv_sem=matrix_recv,
-        device_id={"rcv": twin},
-        device_id_type=MESH,
-    )
-    matrix_copy.start()
+                    matrix[:, j, c, width:LANES, :] = jnp.zeros((pairs, rest, 2 * LANES), jnp.bfloat16)
+                for k in range(chips):
+                    part = refl_ref[j, c, :, k * width : (k + 1) * width]
+                    if rest:
+                        part = jnp.concatenate([part, jnp.zeros((rows, rest), jnp.bfloat16)], 1)
+                    matrix[k // 2, j, c, place, (k % 2) * LANES : (k % 2 + 1) * LANES] = part
+        matrix_copy = pltpu.make_async_remote_copy(
+            src_ref=matrix.at[:, :, :, place, :],
+            dst_ref=matrix.at[:, :, :, place, :],
+            send_sem=matrix_send,
+            recv_sem=matrix_recv,
+            device_id={"rcv": twin},
+            device_id_type=MESH,
+        )
+        matrix_copy.start()
+        matrix_copy.wait()
 
     own_copy.wait()
 
@@ -311,7 +314,7 @@
     lines = first
     for iteration in range(ITERS):
         last = iteration == ITERS - 1
-        forward = convolve(0, lines, 1.0, None if iteration else matrix_copy.wait)
+        forward = convolve(0, lines, 1.0, None if iteration else lay_out)
         up = to_phases(forward, 3.0 * ticks**-0.5)
         back = to_spectrum([u * n for u, n in zip(up, counts)], ticks**-0.5)
         adjoint = convolve(1, back, -1.0, functools.partial(hand_over, 0, up) if last else None)

time: 49.7 us -> 49.7 us (level)
  no operation moved by 1% of the time
where the time goes in v5:
time: 49.7 us; the launch traced here: 49.5 us
  Pallas kernels  48 us (97%)
  local copies, waits for them, and re-layouts  0.91 us (2%)
  between operations  0.68 us (1%)
    pallas_call x1, Pallas kernels, per_device(): pl.pallas_call(functools.partial(iterate, devices, freqs, foci, rows, tic...  46 us
    pallas_call x1, Pallas kernels, per_device(): pl.pallas_call(functools.partial(spread, phases, rows, ticks, count), gri...  1.92 us

profile of v5, /device:TPU:0, one launch (start us, length us, event | category | flops | bytes accessed | tf_op | source)
XLA Modules:
  0.0 49.5 jit_solution(847488757026228962)
XLA Ops:
  0.6 0.0 copy-start.2
  0.6 0.0 copy-start
  0.6 46.0 %shard_map.50.waves_ref = f32[16,2,8,128]{3,2,1,0:T(8,128)} custom-call(bf16[4,2,48,768]{3,2,1,0:T(8,128)(2,1)} %refl_hbm.1, f32[16,48,256]{2,1,0:T(8,128)} %direct_ref.1, s32[16,48]{1,0:T(8,128)} %mute_ref.1), custom_call_target="tpu_custom_call" | custom-call | tf_op jit(solution)/shard_map/pallas_call | solution.py:362
  46.7 0.0 copy-done.2
  46.7 0.0 copy-done
  46.7 0.0 copy-start.1
  46.7 0.9 %copy-done.1 = f32[16,2,8,128]{3,2,1,0:T(8,128)S(1)} copy-done((f32[16,2,8,128]{3,2,1,0:T(8,128)S(1)}, f32[16,2,8,128]{3,2,1,0:T(8,128)}, u32[]{:S(2)}) %copy-start.1) | copy-done | bytes 131096
  47.6 1.9 %shard_map.51 = (f32[16,48,256]{2,1,0:T(8,128)}, f32[16,48,256]{2,1,0:T(8,128)}) custom-call(f32[16,2,8,128]{3,2,1,0:T(8,128)S(1)} %copy-done.1, f32[16,48,256]{2,1,0:T(8,128)S(1)} %copy-done, s32[16,48]{1,0:T(8,128)S(1)} %copy-done.2), custom_call_target="tpu_custom_call" | custom-call | tf_op jit(solution)/shard_map/pallas_call | solution.py:387
Async XLA Ops:
  0.6 46.1 %copy-start.2 = (s32[16,48]{1,0:T(8,128)S(1)}, s32[16,48]{1,0:T(8,128)}, u32[]{:S(2)}) copy-start(s32[16,48]{1,0:T(8,128)} %mute_ref.1) | copy-start | bytes 9220
  0.6 46.1 %copy-start = (f32[16,48,256]{2,1,0:T(8,128)S(1)}, f32[16,48,256]{2,1,0:T(8,128)}, u32[]{:S(2)}) copy-start(f32[16,48,256]{2,1,0:T(8,128)} %direct_ref.1) | copy-start | bytes 2359300
  46.7 0.9 %copy-start.1 = (f32[16,2,8,128]{3,2,1,0:T(8,128)S(1)}, f32[16,2,8,128]{3,2,1,0:T(8,128)}, u32[]{:S(2)}) copy-start(f32[16,2,8,128]{3,2,1,0:T(8,128)} %shard_map.50.waves_ref) | copy-start | bytes 393220
